TPU v7x, 32 devices: a whole 2x2x4 slice. The times are simulated.
32 devices in a mesh: dp: 8 (over z, x), walk: 4 (over y, core).
Axes of the slice: x: 2, y: 2, z: 4, core: 2. Of those that a mesh axis runs over, the one named last changes fastest.
Arguments:
- fields: float32 [512, 65536], P('walk', 'dp'), may hold values from -6 to 6
- sensitivity: bfloat16 [256, 16, 128, 128], P('dp'), may hold values from -0.125 to 0.125
- tile_index: int32 [256, 16], P('dp'), may hold values from 0 to 511
- tile_count: int32 [256], P('dp'), may hold values from 1 to 16, as said below
- observed: float32 [32768], P('dp'), may hold values from -6 to 6
- precision: float32 [32768], P('dp'), may hold values from 0.2 to 4
Outputs:
- fields_next: float32 [512, 65536], P('walk', 'dp')
Inputs may be any that keep to these rules, and one draw needn't show every extreme that they name: `tile_count`: every block of rows uses between 1 and 16 slots, and some block uses all 16; slots at or past the count are ignored.
All inputs are finite; a program needn't handle non-finite values.
Results may differ from a plain program's by a relative error of at most 0.0023.
Values may be sent and summed in bfloat16 or wider, within the bound.
A program may use at most 128 MiB of HBM per device.

v0:
```python
import jax
import jax.numpy as jnp
from jax import lax
from jax.sharding import PartitionSpec as P

WALKERS = 512


def forward(gathered, sensitivity, tile_index, tile_count):
    walkers_here = gathered.shape[0]
    nblocks = sensitivity.shape[0]
    tile_rows = sensitivity.shape[2]
    cell_blocks = gathered.reshape(walkers_here, -1, tile_rows)
    most_live = jnp.max(tile_count)

    def one_slot(slot_id, totals):
        columns = lax.dynamic_index_in_dim(tile_index, slot_id, 1, keepdims=False)
        blocks = jnp.take(cell_blocks, columns, axis=1)
        sensitive = lax.dynamic_index_in_dim(sensitivity, slot_id, 1, keepdims=False)
        product = jnp.einsum("brc,wbc->wbr", sensitive, blocks, preferred_element_type=jnp.float32)
        alive_mask = (slot_id < tile_count)[None, :, None]
        return totals + jnp.where(alive_mask, product, jnp.float32(0.0))

    start_sum = jnp.zeros((walkers_here, nblocks, tile_rows), jnp.float32)
    totals = lax.fori_loop(0, most_live, one_slot, start_sum)
    return totals.reshape(walkers_here, nblocks * tile_rows)


def local(fields, sensitivity, tile_index, tile_count, observed, precision):
    field_bf = fields.astype(jnp.bfloat16)
    gathered = lax.all_gather(field_bf, "dp", axis=1, tiled=True)
    predicted = forward(gathered, sensitivity, tile_index, tile_count)
    pred_sum = lax.psum(jnp.sum(predicted, axis=0), "walk")
    pred_mean = pred_sum / WALKERS
    deviation = (predicted - pred_mean[None, :]).astype(jnp.bfloat16)
    misfit = (precision[None, :] * (predicted - observed[None, :])).astype(jnp.bfloat16)
    partial_rows = lax.dot_general(
        misfit,
        lax.all_gather(deviation, "walk", axis=0, tiled=True),
        (((1,), (1,)), ((), ())),
        preferred_element_type=jnp.float32,
    )
    coupling_mine = lax.psum(partial_rows, "dp") / WALKERS
    squares = lax.psum(jnp.sum(coupling_mine * coupling_mine), "walk")
    spread = jnp.sqrt(squares / (WALKERS * WALKERS) + 1e-06)
    weights = (8.0 * coupling_mine / (WALKERS * spread)).astype(jnp.bfloat16)
    update = jnp.dot(
        weights,
        lax.all_gather(field_bf, "walk", axis=0, tiled=True),
        preferred_element_type=jnp.float32,
    )
    return fields - update


def solution(mesh):
    placed = (P("walk", "dp"), P("dp", None, None, None), P("dp", None), P("dp"), P("dp"), P("dp"))
    return jax.shard_map(
        local, mesh=mesh, in_specs=placed, out_specs=P("walk", "dp"), check_vma=False
    )
```

profile of v0, /device:TPU:0, one launch (start us, length us, event | category | flops | bytes accessed | tf_op | source)
XLA Modules:
  0.0 632.2 jit_solution(5999888927857076047)
XLA Ops:
  6.5 4.6 copy.11
  11.3 0.7 reduce_max.9
  11.9 229.7 %all-gather.4.cloned.1.call-done = bf16[128,65536]{0,1:T(8,128)(2,1)} async-done(((bf16[128,8192]{0,1:T(8,128)(2,1)}), bf16[128,65536]{0,1:T(8,128)(2,1)}) %all-gather.4.cloned.1.call-update) | async-done | bytes 16777232 | tf_op jit(solution)/shard_map/all_gather | solution.py:31
  241.7 22.4 %copy.12 = bf16[128,512,128]{2,0,1:T(8,128)(2,1)} copy(bf16[128,512,128]{0,2,1:T(8,128)(2,1)} %bitcast.37) | data formatting | bytes 33554432 | tf_op jit(solution)/shard_map/while | solution.py:25
  264.3 167.2 %while.10 = (s32[]{:T(128)}, f32[128,32,128]{2,0,1:T(8,128)S(1)}, s32[]{:T(128)}, s32[32]{0:T(128)S(1)}, s32[32,16]{0,1:T(8,128)}, /*index=5*/bf16[128,512,128]{...) while((s32[]{:T(128)}, f32[128,32,128]{2,0,1:T(8,128)S(1)}, ...), condition=%wide.region_2.3_spmd, body=%wide.region_1.2_spmd.sunk | while | flops 135791840 | bytes 8393619 | solution.py:25
  264.9 0.7 and_bitcast_fusion.2
  265.6 6.5 %gather_fusion = bf16[32,128,128]{2,1,0:T(8,128)(2,1)S(1)} fusion(bf16[128,512,128]{2,0,1:T(8,128)(2,1)} %get-tuple-element.156, s32[1024]{0:T(1024)S(1)} %pad_clamp_fusion.2), kind=kCustom, calls=%fused_computation.clone.1 | custom fusion | bytes 2097280 | tf_op jit(solution)/shard_map/while/body/jit(_take)/gather | solution.py:18
  272.2 2.5 bitcast_add_fusion.2
  275.3 0.7 and_bitcast_fusion.2
  276.1 6.5 %gather_fusion = bf16[32,128,128]{2,1,0:T(8,128)(2,1)S(1)} fusion(bf16[128,512,128]{2,0,1:T(8,128)(2,1)} %get-tuple-element.156, s32[1024]{0:T(1024)S(1)} %pad_clamp_fusion.2), kind=kCustom, calls=%fused_computation.clone.1 | custom fusion | bytes 2097280 | tf_op jit(solution)/shard_map/while/body/jit(_take)/gather | solution.py:18
  282.6 2.5 bitcast_add_fusion.2
  285.8 0.7 and_bitcast_fusion.2
  286.5 6.5 %gather_fusion = bf16[32,128,128]{2,1,0:T(8,128)(2,1)S(1)} fusion(bf16[128,512,128]{2,0,1:T(8,128)(2,1)} %get-tuple-element.156, s32[1024]{0:T(1024)S(1)} %pad_clamp_fusion.2), kind=kCustom, calls=%fused_computation.clone.1 | custom fusion | bytes 2097280 | tf_op jit(solution)/shard_map/while/body/jit(_take)/gather | solution.py:18
  293.0 2.5 bitcast_add_fusion.2
  296.2 0.7 and_bitcast_fusion.2
  296.9 6.5 %gather_fusion = bf16[32,128,128]{2,1,0:T(8,128)(2,1)S(1)} fusion(bf16[128,512,128]{2,0,1:T(8,128)(2,1)} %get-tuple-element.156, s32[1024]{0:T(1024)S(1)} %pad_clamp_fusion.2), kind=kCustom, calls=%fused_computation.clone.1 | custom fusion | bytes 2097280 | tf_op jit(solution)/shard_map/while/body/jit(_take)/gather | solution.py:18
  303.4 2.5 bitcast_add_fusion.2
  306.6 0.7 and_bitcast_fusion.2
  307.3 6.5 %gather_fusion = bf16[32,128,128]{2,1,0:T(8,128)(2,1)S(1)} fusion(bf16[128,512,128]{2,0,1:T(8,128)(2,1)} %get-tuple-element.156, s32[1024]{0:T(1024)S(1)} %pad_clamp_fusion.2), kind=kCustom, calls=%fused_computation.clone.1 | custom fusion | bytes 2097280 | tf_op jit(solution)/shard_map/while/body/jit(_take)/gather | solution.py:18
  313.8 2.5 bitcast_add_fusion.2
  317.0 0.7 and_bitcast_fusion.2
  317.7 6.5 %gather_fusion = bf16[32,128,128]{2,1,0:T(8,128)(2,1)S(1)} fusion(bf16[128,512,128]{2,0,1:T(8,128)(2,1)} %get-tuple-element.156, s32[1024]{0:T(1024)S(1)} %pad_clamp_fusion.2), kind=kCustom, calls=%fused_computation.clone.1 | custom fusion | bytes 2097280 | tf_op jit(solution)/shard_map/while/body/jit(_take)/gather | solution.py:18
  324.2 2.5 bitcast_add_fusion.2
  327.4 0.7 and_bitcast_fusion.2
  328.1 6.5 %gather_fusion = bf16[32,128,128]{2,1,0:T(8,128)(2,1)S(1)} fusion(bf16[128,512,128]{2,0,1:T(8,128)(2,1)} %get-tuple-element.156, s32[1024]{0:T(1024)S(1)} %pad_clamp_fusion.2), kind=kCustom, calls=%fused_computation.clone.1 | custom fusion | bytes 2097280 | tf_op jit(solution)/shard_map/while/body/jit(_take)/gather | solution.py:18
  334.6 2.5 bitcast_add_fusion.2
  337.8 0.7 and_bitcast_fusion.2
  338.5 6.5 %gather_fusion = bf16[32,128,128]{2,1,0:T(8,128)(2,1)S(1)} fusion(bf16[128,512,128]{2,0,1:T(8,128)(2,1)} %get-tuple-element.156, s32[1024]{0:T(1024)S(1)} %pad_clamp_fusion.2), kind=kCustom, calls=%fused_computation.clone.1 | custom fusion | bytes 2097280 | tf_op jit(solution)/shard_map/while/body/jit(_take)/gather | solution.py:18
  345.0 2.5 bitcast_add_fusion.2
  348.2 0.7 and_bitcast_fusion.2
  348.9 6.5 %gather_fusion = bf16[32,128,128]{2,1,0:T(8,128)(2,1)S(1)} fusion(bf16[128,512,128]{2,0,1:T(8,128)(2,1)} %get-tuple-element.156, s32[1024]{0:T(1024)S(1)} %pad_clamp_fusion.2), kind=kCustom, calls=%fused_computation.clone.1 | custom fusion | bytes 2097280 | tf_op jit(solution)/shard_map/while/body/jit(_take)/gather | solution.py:18
  355.4 2.5 bitcast_add_fusion.2
  358.6 0.7 and_bitcast_fusion.2
  359.3 6.5 %gather_fusion = bf16[32,128,128]{2,1,0:T(8,128)(2,1)S(1)} fusion(bf16[128,512,128]{2,0,1:T(8,128)(2,1)} %get-tuple-element.156, s32[1024]{0:T(1024)S(1)} %pad_clamp_fusion.2), kind=kCustom, calls=%fused_computation.clone.1 | custom fusion | bytes 2097280 | tf_op jit(solution)/shard_map/while/body/jit(_take)/gather | solution.py:18
  365.9 2.5 bitcast_add_fusion.2
  369.0 0.7 and_bitcast_fusion.2
  369.7 6.5 %gather_fusion = bf16[32,128,128]{2,1,0:T(8,128)(2,1)S(1)} fusion(bf16[128,512,128]{2,0,1:T(8,128)(2,1)} %get-tuple-element.156, s32[1024]{0:T(1024)S(1)} %pad_clamp_fusion.2), kind=kCustom, calls=%fused_computation.clone.1 | custom fusion | bytes 2097280 | tf_op jit(solution)/shard_map/while/body/jit(_take)/gather | solution.py:18
  376.3 2.5 bitcast_add_fusion.2
  379.4 0.7 and_bitcast_fusion.2
  380.1 6.5 %gather_fusion = bf16[32,128,128]{2,1,0:T(8,128)(2,1)S(1)} fusion(bf16[128,512,128]{2,0,1:T(8,128)(2,1)} %get-tuple-element.156, s32[1024]{0:T(1024)S(1)} %pad_clamp_fusion.2), kind=kCustom, calls=%fused_computation.clone.1 | custom fusion | bytes 2097280 | tf_op jit(solution)/shard_map/while/body/jit(_take)/gather | solution.py:18
  386.7 2.5 bitcast_add_fusion.2
  389.8 0.7 and_bitcast_fusion.2
  390.5 6.5 %gather_fusion = bf16[32,128,128]{2,1,0:T(8,128)(2,1)S(1)} fusion(bf16[128,512,128]{2,0,1:T(8,128)(2,1)} %get-tuple-element.156, s32[1024]{0:T(1024)S(1)} %pad_clamp_fusion.2), kind=kCustom, calls=%fused_computation.clone.1 | custom fusion | bytes 2097280 | tf_op jit(solution)/shard_map/while/body/jit(_take)/gather | solution.py:18
  397.1 2.5 bitcast_add_fusion.2
  400.2 0.7 and_bitcast_fusion.2
  401.0 6.5 %gather_fusion = bf16[32,128,128]{2,1,0:T(8,128)(2,1)S(1)} fusion(bf16[128,512,128]{2,0,1:T(8,128)(2,1)} %get-tuple-element.156, s32[1024]{0:T(1024)S(1)} %pad_clamp_fusion.2), kind=kCustom, calls=%fused_computation.clone.1 | custom fusion | bytes 2097280 | tf_op jit(solution)/shard_map/while/body/jit(_take)/gather | solution.py:18
  407.5 2.5 bitcast_add_fusion.2
  410.7 0.7 and_bitcast_fusion.2
  411.4 6.5 %gather_fusion = bf16[32,128,128]{2,1,0:T(8,128)(2,1)S(1)} fusion(bf16[128,512,128]{2,0,1:T(8,128)(2,1)} %get-tuple-element.156, s32[1024]{0:T(1024)S(1)} %pad_clamp_fusion.2), kind=kCustom, calls=%fused_computation.clone.1 | custom fusion | bytes 2097280 | tf_op jit(solution)/shard_map/while/body/jit(_take)/gather | solution.py:18
  417.9 2.5 bitcast_add_fusion.2
  421.1 0.7 and_bitcast_fusion.2
  421.8 6.5 %gather_fusion = bf16[32,128,128]{2,1,0:T(8,128)(2,1)S(1)} fusion(bf16[128,512,128]{2,0,1:T(8,128)(2,1)} %get-tuple-element.156, s32[1024]{0:T(1024)S(1)} %pad_clamp_fusion.2), kind=kCustom, calls=%fused_computation.clone.1 | custom fusion | bytes 2097280 | tf_op jit(solution)/shard_map/while/body/jit(_take)/gather | solution.py:18
  428.3 2.5 bitcast_add_fusion.2
  431.5 1.9 copy.14
  433.5 10.5 %psum.21 = f32[4096]{0:T(1024)S(1)} all-reduce(f32[4096]{0:T(1024)S(1)} %bitcast.38), channel_id=1, replica_groups=mesh['dp'=8,'walk'=4] {'walk'}, use_global_device_ids=true, to_apply=%region_4.5 | all-reduce | flops 4096 | bytes 32768 | tf_op jit(solution)/shard_map/psum | solution.py:33
  444.0 4.5 fusion.10
  448.5 33.1 %all-gather.6.cloned.1.call-done = bf16[512,4096]{0,1:T(8,128)(2,1)} async-done(((bf16[128,4096]{0,1:T(8,128)(2,1)}), bf16[512,4096]{0,1:T(8,128)(2,1)}) %all-gather.6.cloned.1.call-update) | async-done | bytes 4194320 | tf_op jit(solution)/shard_map/all_gather | solution.py:39
  481.6 3.6 fusion.14
  485.3 0.5 all-gather.8.cloned.1.call-update
  485.8 70.1 %all-reduce.2.cloned.1.call-done = f32[128,512]{1,0:T(8,128)} async-done(((f32[128,512]{1,0:T(8,128)}), f32[128,512]{1,0:T(8,128)}) %all-reduce.2.cloned.1.call-update) | async-done | bytes 262160 | tf_op jit(solution)/shard_map/psum | solution.py:43
  556.0 1.6 multiply_reduce_fusion
  557.6 6.3 psum.23
  564.5 51.7 %all-gather.8.cloned.1.call-done = bf16[512,8192]{0,1:T(8,128)(2,1)} async-done(((bf16[128,8192]{0,1:T(8,128)(2,1)}), bf16[512,8192]{0,1:T(8,128)(2,1)}) %all-gather.8.cloned.1.call-update) | async-done | bytes 8388624 | tf_op jit(solution)/shard_map/all_gather | solution.py:49
  616.2 9.5 %convolution_subtract_fusion = f32[128,8192]{1,0:T(8,128)} fusion(f32[128,8192]{1,0:T(8,128)} %param.8, bf16[512,8192]{0,1:T(8,128)(2,1)} %all-gather.8.cloned.1.call-done, f32[128,512]{1,0:T(8,128)} %all-reduce.2.cloned.1.call-done, f32[]{:T(128)S(6)} %mul.25), kind=kOutput, calls=%fused_computation.14 | convolution fusion | flops 1074987008 | bytes 17039364 | tf_op jit(solution)/shard_map/dot_general | solution.py:47
  (48 shorter events, 0.7 us)
Async XLA Ops:
  6.5 4.7 copy-start.2
  6.5 235.1 %all-gather.4.cloned.1.call-start = ((), (), s32[]{:S(2)}) async-start(), calls=%async_computation | async-start | bytes 18874368 | tf_op jit(solution)/shard_map/all_gather | solution.py:31
  11.2 470.4 %all-gather.6.cloned.1.call-start = ((), (), s32[]{:S(2)}) async-start(), calls=%async_computation.1 | async-start | bytes 5242880 | tf_op jit(solution)/shard_map/all_gather | solution.py:39
  431.5 12.5 %copy-start = (f32[4096]{0:T(1024)S(1)}, f32[4096]{0:T(1024)}, u32[]{:S(2)}) copy-start(f32[4096]{0:T(1024)} %param.12) | copy-start | bytes 49156
  431.5 12.5 %copy-start.1 = (f32[4096]{0:T(1024)S(1)}, f32[4096]{0:T(1024)}, u32[]{:S(2)}) copy-start(f32[4096]{0:T(1024)} %param.13) | copy-start | bytes 49156
  448.5 107.5 %all-reduce.2.cloned.1.call-start = ((), (), s32[]{:S(2)}) async-start(), calls=%async_computation.2 | async-start | bytes 524288 | tf_op jit(solution)/shard_map/psum | solution.py:43
  485.3 130.9 %all-gather.8.cloned.1.call-start = ((), (), s32[]{:S(2)}) async-start(), calls=%async_computation.3 | async-start | bytes 10485760 | tf_op jit(solution)/shard_map/all_gather | solution.py:49
Sparse Core Ops, SparseCore 0:
  11.3 230.2 all-gather.3
  448.6 32.9 all-gather.5
  485.4 70.5 all-reduce.1
  557.5 58.6 all-gather.7
where the time goes:
time: 635 us; the launch traced here: 632 us
  waiting for transfers between devices  385 us (61%)
  local copies, waits for them, and re-layouts  133 us (21%)
  matrix products  53.6 us (8%)
  other arithmetic  18.3 us (3%)
  blocking collectives  16.7 us (3%)
  between operations  13.8 us (2%)
  loops' own time  11 us (2%)
    all_gather x1, waiting for transfers between devices, local(): gathered = lax.all_gather(field_bf, 'dp', axis=1, tiled=True)  230 us
    gather x16, local copies, waits for them, and re-layouts, one_slot(): blocks = jnp.take(cell_blocks, columns, axis=1)  104 us
    psum x1, waiting for transfers between devices, local(): coupling_mine = lax.psum(partial_rows, 'dp') / WALKERS  70.1 us
    all_gather x1, waiting for transfers between devices, local(): lax.all_gather(field_bf, 'walk', axis=0, tiled=True)  51.7 us
    dot_general x16, matrix products, one_slot(): jnp.einsum('brc,wbc->wbr', sensitive, blocks, preferred_element_type=jnp....  40.4 us
    all_gather x1, waiting for transfers between devices, local(): lax.all_gather(deviation, 'walk', axis=0, tiled=True)  33.1 us
    while x2, local copies, waits for them, and re-layouts, forward(): totals = lax.fori_loop(0, most_live, one_slot, start_sum)  24.3 us
  transfers between devices with their start and end apart: 4, of which 4 were waited for; matrix products, arithmetic and copies ran while one was open for 0% of the time, Pallas kernels for 0%

commit v1 on v0

--- a/solution.py
+++ b/solution.py
@@ -40,7 +40,7 @@
         (((1,), (1,)), ((), ())),
         preferred_element_type=jnp.float32,
     )
-    coupling_mine = lax.psum(partial_rows, "dp") / WALKERS
+    coupling_mine = lax.all_gather(partial_rows, "dp").sum(axis=0) / WALKERS
     squares = lax.psum(jnp.sum(coupling_mine * coupling_mine), "walk")
     spread = jnp.sqrt(squares / (WALKERS * WALKERS) + 1e-06)
     weights = (8.0 * coupling_mine / (WALKERS * spread)).astype(jnp.bfloat16)

time: 635 us -> 613 us (0.965)
  waiting for transfers between devices: 385 us -> 362 us
    psum x1 -> x0, waiting for transfers between devices: 70.1 us -> none  [local(): coupling_mine = lax.psum(partial_rows, 'dp') / WALKERS]
    all_gather x0 -> x1, waiting for transfers between devices: none -> 48.9 us  [local(): coupling_mine = lax.all_gather(partial_rows, 'dp').sum(axis=0) / WALKERS]
  transfers between devices with their start and end apart: 4 -> 4, of which waited for: 4 -> 4; matrix products, arithmetic and copies ran while one was open for 0% -> 1% of each run, Pallas kernels for 0% -> 0%
where the time goes in v1:
time: 613 us; the launch traced here: 610 us
  waiting for transfers between devices  362 us (59%)
  local copies, waits for them, and re-layouts  134 us (22%)
  matrix products  53.5 us (9%)
  other arithmetic  19.2 us (3%)
  blocking collectives  16.8 us (3%)
  between operations  13.8 us (2%)
  loops' own time  11 us (2%)
    all_gather x1, waiting for transfers between devices, local(): gathered = lax.all_gather(field_bf, 'dp', axis=1, tiled=True)  229 us
    gather x16, local copies, waits for them, and re-layouts, one_slot(): blocks = jnp.take(cell_blocks, columns, axis=1)  104 us
    all_gather x1, waiting for transfers between devices, local(): lax.all_gather(field_bf, 'walk', axis=0, tiled=True)  49.9 us
    all_gather x1, waiting for transfers between devices, local(): coupling_mine = lax.all_gather(partial_rows, 'dp').sum(axis=0) / WALKERS  48.9 us
    dot_general x16, matrix products, one_slot(): jnp.einsum('brc,wbc->wbr', sensitive, blocks, preferred_element_type=jnp....  40.4 us
    all_gather x1, waiting for transfers between devices, local(): lax.all_gather(deviation, 'walk', axis=0, tiled=True)  33.1 us
    while x2, local copies, waits for them, and re-layouts, forward(): totals = lax.fori_loop(0, most_live, one_slot, start_sum)  24.3 us
  transfers between devices with their start and end apart: 4, of which 4 were waited for; matrix products, arithmetic and copies ran while one was open for 1% of the time, Pallas kernels for 0%

profile of v1, /device:TPU:0, one launch (start us, length us, event | category | flops | bytes accessed | tf_op | source)
XLA Modules:
  0.0 610.0 jit_solution(11276953485882545837)
XLA Ops:
  6.5 4.6 copy.15
  11.8 0.7 reduce_max.9
  12.5 229.2 %all-gather.6.cloned.1.call-done = bf16[128,65536]{0,1:T(8,128)(2,1)} async-done(((bf16[128,8192]{0,1:T(8,128)(2,1)}), bf16[128,65536]{0,1:T(8,128)(2,1)}) %all-gather.6.cloned.1.call-update) | async-done | bytes 16777232 | tf_op jit(solution)/shard_map/all_gather | solution.py:31
  241.6 22.4 %copy.16 = bf16[128,512,128]{2,0,1:T(8,128)(2,1)} copy(bf16[128,512,128]{0,2,1:T(8,128)(2,1)} %bitcast.38) | data formatting | bytes 33554432 | tf_op jit(solution)/shard_map/while | solution.py:25
  264.3 167.2 %while.10 = (s32[]{:T(128)}, f32[128,32,128]{2,0,1:T(8,128)S(1)}, s32[]{:T(128)}, s32[32]{0:T(128)S(1)}, s32[32,16]{0,1:T(8,128)}, /*index=5*/bf16[128,512,128]{...) while((s32[]{:T(128)}, f32[128,32,128]{2,0,1:T(8,128)S(1)}, ...), condition=%wide.region_2.3_spmd, body=%wide.region_1.2_spmd.sunk | while | flops 135791840 | bytes 8393619 | solution.py:25
  264.9 0.7 and_bitcast_fusion.2
  265.6 6.5 %gather_fusion = bf16[32,128,128]{2,1,0:T(8,128)(2,1)S(1)} fusion(bf16[128,512,128]{2,0,1:T(8,128)(2,1)} %get-tuple-element.163, s32[1024]{0:T(1024)S(1)} %pad_clamp_fusion.2), kind=kCustom, calls=%fused_computation.clone.1 | custom fusion | bytes 2097280 | tf_op jit(solution)/shard_map/while/body/jit(_take)/gather | solution.py:18
  272.2 2.5 bitcast_add_fusion.2
  275.3 0.7 and_bitcast_fusion.2
  276.0 6.5 %gather_fusion = bf16[32,128,128]{2,1,0:T(8,128)(2,1)S(1)} fusion(bf16[128,512,128]{2,0,1:T(8,128)(2,1)} %get-tuple-element.163, s32[1024]{0:T(1024)S(1)} %pad_clamp_fusion.2), kind=kCustom, calls=%fused_computation.clone.1 | custom fusion | bytes 2097280 | tf_op jit(solution)/shard_map/while/body/jit(_take)/gather | solution.py:18
  282.6 2.5 bitcast_add_fusion.2
  285.7 0.7 and_bitcast_fusion.2
  286.5 6.5 %gather_fusion = bf16[32,128,128]{2,1,0:T(8,128)(2,1)S(1)} fusion(bf16[128,512,128]{2,0,1:T(8,128)(2,1)} %get-tuple-element.163, s32[1024]{0:T(1024)S(1)} %pad_clamp_fusion.2), kind=kCustom, calls=%fused_computation.clone.1 | custom fusion | bytes 2097280 | tf_op jit(solution)/shard_map/while/body/jit(_take)/gather | solution.py:18
  293.0 2.5 bitcast_add_fusion.2
  296.1 0.7 and_bitcast_fusion.2
  296.9 6.5 %gather_fusion = bf16[32,128,128]{2,1,0:T(8,128)(2,1)S(1)} fusion(bf16[128,512,128]{2,0,1:T(8,128)(2,1)} %get-tuple-element.163, s32[1024]{0:T(1024)S(1)} %pad_clamp_fusion.2), kind=kCustom, calls=%fused_computation.clone.1 | custom fusion | bytes 2097280 | tf_op jit(solution)/shard_map/while/body/jit(_take)/gather | solution.py:18
  303.4 2.5 bitcast_add_fusion.2
  306.6 0.7 and_bitcast_fusion.2
  307.3 6.5 %gather_fusion = bf16[32,128,128]{2,1,0:T(8,128)(2,1)S(1)} fusion(bf16[128,512,128]{2,0,1:T(8,128)(2,1)} %get-tuple-element.163, s32[1024]{0:T(1024)S(1)} %pad_clamp_fusion.2), kind=kCustom, calls=%fused_computation.clone.1 | custom fusion | bytes 2097280 | tf_op jit(solution)/shard_map/while/body/jit(_take)/gather | solution.py:18
  313.8 2.5 bitcast_add_fusion.2
  317.0 0.7 and_bitcast_fusion.2
  317.7 6.5 %gather_fusion = bf16[32,128,128]{2,1,0:T(8,128)(2,1)S(1)} fusion(bf16[128,512,128]{2,0,1:T(8,128)(2,1)} %get-tuple-element.163, s32[1024]{0:T(1024)S(1)} %pad_clamp_fusion.2), kind=kCustom, calls=%fused_computation.clone.1 | custom fusion | bytes 2097280 | tf_op jit(solution)/shard_map/while/body/jit(_take)/gather | solution.py:18
  324.2 2.5 bitcast_add_fusion.2
  327.4 0.7 and_bitcast_fusion.2
  328.1 6.5 %gather_fusion = bf16[32,128,128]{2,1,0:T(8,128)(2,1)S(1)} fusion(bf16[128,512,128]{2,0,1:T(8,128)(2,1)} %get-tuple-element.163, s32[1024]{0:T(1024)S(1)} %pad_clamp_fusion.2), kind=kCustom, calls=%fused_computation.clone.1 | custom fusion | bytes 2097280 | tf_op jit(solution)/shard_map/while/body/jit(_take)/gather | solution.py:18
  334.6 2.5 bitcast_add_fusion.2
  337.8 0.7 and_bitcast_fusion.2
  338.5 6.5 %gather_fusion = bf16[32,128,128]{2,1,0:T(8,128)(2,1)S(1)} fusion(bf16[128,512,128]{2,0,1:T(8,128)(2,1)} %get-tuple-element.163, s32[1024]{0:T(1024)S(1)} %pad_clamp_fusion.2), kind=kCustom, calls=%fused_computation.clone.1 | custom fusion | bytes 2097280 | tf_op jit(solution)/shard_map/while/body/jit(_take)/gather | solution.py:18
  345.0 2.5 bitcast_add_fusion.2
  348.2 0.7 and_bitcast_fusion.2
  348.9 6.5 %gather_fusion = bf16[32,128,128]{2,1,0:T(8,128)(2,1)S(1)} fusion(bf16[128,512,128]{2,0,1:T(8,128)(2,1)} %get-tuple-element.163, s32[1024]{0:T(1024)S(1)} %pad_clamp_fusion.2), kind=kCustom, calls=%fused_computation.clone.1 | custom fusion | bytes 2097280 | tf_op jit(solution)/shard_map/while/body/jit(_take)/gather | solution.py:18
  355.4 2.5 bitcast_add_fusion.2
  358.6 0.7 and_bitcast_fusion.2
  359.3 6.5 %gather_fusion = bf16[32,128,128]{2,1,0:T(8,128)(2,1)S(1)} fusion(bf16[128,512,128]{2,0,1:T(8,128)(2,1)} %get-tuple-element.163, s32[1024]{0:T(1024)S(1)} %pad_clamp_fusion.2), kind=kCustom, calls=%fused_computation.clone.1 | custom fusion | bytes 2097280 | tf_op jit(solution)/shard_map/while/body/jit(_take)/gather | solution.py:18
  365.9 2.5 bitcast_add_fusion.2
  369.0 0.7 and_bitcast_fusion.2
  369.7 6.5 %gather_fusion = bf16[32,128,128]{2,1,0:T(8,128)(2,1)S(1)} fusion(bf16[128,512,128]{2,0,1:T(8,128)(2,1)} %get-tuple-element.163, s32[1024]{0:T(1024)S(1)} %pad_clamp_fusion.2), kind=kCustom, calls=%fused_computation.clone.1 | custom fusion | bytes 2097280 | tf_op jit(solution)/shard_map/while/body/jit(_take)/gather | solution.py:18
  376.3 2.5 bitcast_add_fusion.2
  379.4 0.7 and_bitcast_fusion.2
  380.1 6.5 %gather_fusion = bf16[32,128,128]{2,1,0:T(8,128)(2,1)S(1)} fusion(bf16[128,512,128]{2,0,1:T(8,128)(2,1)} %get-tuple-element.163, s32[1024]{0:T(1024)S(1)} %pad_clamp_fusion.2), kind=kCustom, calls=%fused_computation.clone.1 | custom fusion | bytes 2097280 | tf_op jit(solution)/shard_map/while/body/jit(_take)/gather | solution.py:18
  386.7 2.5 bitcast_add_fusion.2
  389.8 0.7 and_bitcast_fusion.2
  390.5 6.5 %gather_fusion = bf16[32,128,128]{2,1,0:T(8,128)(2,1)S(1)} fusion(bf16[128,512,128]{2,0,1:T(8,128)(2,1)} %get-tuple-element.163, s32[1024]{0:T(1024)S(1)} %pad_clamp_fusion.2), kind=kCustom, calls=%fused_computation.clone.1 | custom fusion | bytes 2097280 | tf_op jit(solution)/shard_map/while/body/jit(_take)/gather | solution.py:18
  397.1 2.5 bitcast_add_fusion.2
  400.2 0.7 and_bitcast_fusion.2
  400.9 6.5 %gather_fusion = bf16[32,128,128]{2,1,0:T(8,128)(2,1)S(1)} fusion(bf16[128,512,128]{2,0,1:T(8,128)(2,1)} %get-tuple-element.163, s32[1024]{0:T(1024)S(1)} %pad_clamp_fusion.2), kind=kCustom, calls=%fused_computation.clone.1 | custom fusion | bytes 2097280 | tf_op jit(solution)/shard_map/while/body/jit(_take)/gather | solution.py:18
  407.5 2.5 bitcast_add_fusion.2
  410.6 0.7 and_bitcast_fusion.2
  411.4 6.5 %gather_fusion = bf16[32,128,128]{2,1,0:T(8,128)(2,1)S(1)} fusion(bf16[128,512,128]{2,0,1:T(8,128)(2,1)} %get-tuple-element.163, s32[1024]{0:T(1024)S(1)} %pad_clamp_fusion.2), kind=kCustom, calls=%fused_computation.clone.1 | custom fusion | bytes 2097280 | tf_op jit(solution)/shard_map/while/body/jit(_take)/gather | solution.py:18
  417.9 2.5 bitcast_add_fusion.2
  421.1 0.7 and_bitcast_fusion.2
  421.8 6.5 %gather_fusion = bf16[32,128,128]{2,1,0:T(8,128)(2,1)S(1)} fusion(bf16[128,512,128]{2,0,1:T(8,128)(2,1)} %get-tuple-element.163, s32[1024]{0:T(1024)S(1)} %pad_clamp_fusion.2), kind=kCustom, calls=%fused_computation.clone.1 | custom fusion | bytes 2097280 | tf_op jit(solution)/shard_map/while/body/jit(_take)/gather | solution.py:18
  428.3 2.5 bitcast_add_fusion.2
  431.4 1.9 copy.18
  433.5 10.5 %psum.14 = f32[4096]{0:T(1024)S(1)} all-reduce(f32[4096]{0:T(1024)S(1)} %bitcast.40), channel_id=1, replica_groups=mesh['dp'=8,'walk'=4] {'walk'}, use_global_device_ids=true, to_apply=%region_4.5 | all-reduce | flops 4096 | bytes 32768 | tf_op jit(solution)/shard_map/psum | solution.py:33
  444.0 4.5 fusion.10
  448.5 33.1 %all-gather.8.cloned.1.call-done = bf16[512,4096]{0,1:T(8,128)(2,1)} async-done(((bf16[128,4096]{0,1:T(8,128)(2,1)}), bf16[512,4096]{0,1:T(8,128)(2,1)}) %all-gather.8.cloned.1.call-update) | async-done | bytes 4194320 | tf_op jit(solution)/shard_map/all_gather | solution.py:39
  481.6 3.7 fusion.14
  485.8 48.9 %all-gather.12.cloned.1.call-done = f32[1024,512]{1,0:T(8,128)} async-done(((f32[128,512]{1,0:T(8,128)}), f32[1024,512]{1,0:T(8,128)}) %all-gather.12.cloned.1.call-update) | async-done | bytes 2097168 | tf_op jit(solution)/shard_map/all_gather | solution.py:43
  534.7 1.8 reduce_sum.31
  536.5 0.7 multiply_reduce_fusion
  537.2 6.3 %psum.15 = f32[]{:T(128)} all-reduce(f32[]{:T(128)} %multiply_reduce_fusion), channel_id=1, replica_groups=mesh['dp'=8,'walk'=4] {'walk'}, use_global_device_ids=true, to_apply=%region_7.8 | all-reduce | flops 1 | bytes 8 | tf_op jit(solution)/shard_map/psum | solution.py:44
  544.2 49.9 %all-gather.10.cloned.1.call-done = bf16[512,8192]{0,1:T(8,128)(2,1)} async-done(((bf16[128,8192]{0,1:T(8,128)(2,1)}), bf16[512,8192]{0,1:T(8,128)(2,1)}) %all-gather.10.cloned.1.call-update) | async-done | bytes 8388624 | tf_op jit(solution)/shard_map/all_gather | solution.py:49
  594.0 9.4 %convolution_subtract_fusion = f32[128,8192]{1,0:T(8,128)} fusion(f32[128,8192]{1,0:T(8,128)} %param.8, bf16[512,8192]{0,1:T(8,128)(2,1)} %all-gather.10.cloned.1.call-done, f32[128,512]{1,0:T(8,128)S(1)} %reduce_sum.31, f32[]{:T(128)S(6)} %mul.25), kind=kOutput, calls=%fused_computation.14 | convolution fusion | flops 1074987008 | bytes 17039364 | tf_op jit(solution)/shard_map/dot_general | solution.py:47
  (49 shorter events, 1.8 us)
Async XLA Ops:
  6.5 235.1 %all-gather.6.cloned.1.call-start = ((), (), s32[]{:S(2)}) async-start(), calls=%async_computation | async-start | bytes 18874368 | tf_op jit(solution)/shard_map/all_gather | solution.py:31
  11.2 0.7 copy-start.2
  11.2 470.4 %all-gather.8.cloned.1.call-start = ((), (), s32[]{:S(2)}) async-start(), calls=%async_computation.1 | async-start | bytes 5242880 | tf_op jit(solution)/shard_map/all_gather | solution.py:39
  433.3 10.6 %copy-start = (f32[4096]{0:T(1024)S(1)}, f32[4096]{0:T(1024)}, u32[]{:S(2)}) copy-start(f32[4096]{0:T(1024)} %param.12) | copy-start | bytes 49156
  433.3 10.6 %copy-start.1 = (f32[4096]{0:T(1024)S(1)}, f32[4096]{0:T(1024)}, u32[]{:S(2)}) copy-start(f32[4096]{0:T(1024)} %param.13) | copy-start | bytes 49156
  448.4 86.3 %all-gather.12.cloned.1.call-start = ((), (), s32[]{:S(2)}) async-start(), calls=%async_computation.3 | async-start | bytes 2359296 | tf_op jit(solution)/shard_map/all_gather | solution.py:43
  485.3 108.8 %all-gather.10.cloned.1.call-start = ((), (), s32[]{:S(2)}) async-start(), calls=%async_computation.2 | async-start | bytes 10485760 | tf_op jit(solution)/shard_map/all_gather | solution.py:49
Sparse Core Ops, SparseCore 0:
  11.3 230.2 all-gather.5
  448.6 32.9 all-gather.7
  485.4 49.2 all-gather.11
  536.1 57.8 all-gather.9
